TPU v7x, 512 devices: a whole 4x8x8 slice. The times are simulated.
512 devices in a mesh: frame: 64 (over y, x, core), head: 8 (over z).
Axes of the slice: x: 4, y: 8, z: 8, core: 2. Of those that a mesh axis runs over, the one named last changes fastest.
Arguments:
- queries: bfloat16 [16384, 3072], P('frame', 'head')
- keys: bfloat16 [16384, 3072], P('frame', 'head')
- values: bfloat16 [16384, 3072], P('frame', 'head'), may hold values from -6 to 6
- text_keys: bfloat16 [256, 3072], P('frame', 'head'), may hold values from -6 to 6
- text_values: bfloat16 [256, 3072], P('frame', 'head'), may hold values from -6 to 6
- head_kinds: int32 [24], replicated, may hold values 0 or 1
- text_count: int32 [1], replicated, may hold values from 64 to 256
- w_out: bfloat16 [3072, 3072], P('head', 'frame'), may hold values from -0.109375 to 0.109375
Outputs:
- projected: bfloat16 [16384, 3072], P(('frame', 'head'))
All inputs are finite; a program needn't handle non-finite values.
Results may differ from a plain program's by a relative error of at most 0.022.
Values may be sent and summed in bfloat16 or wider, within the bound.
A program may use at most 64 MiB of HBM per device.

v0:
```python
import jax
import jax.numpy as jnp
from jax import lax
from jax.sharding import PartitionSpec as P

HD = 128


def soft_weights(scores):
    top = jnp.max(scores, axis=-1, keepdims=True)
    expo = jnp.exp(scores - top)
    return (expo / jnp.sum(expo, axis=-1, keepdims=True)).astype(jnp.bfloat16)


def spatial_attend(query, key_all, value_all, live):
    scores = jnp.einsum(
        "qhd,khd->hqk", query, key_all, preferred_element_type=jnp.float32
    ) * HD ** (-0.5)
    scores = jnp.where(live[None, None, :], scores, -1e30)
    weights = soft_weights(scores)
    return jnp.einsum("hqk,khd->qhd", weights, value_all, preferred_element_type=jnp.float32)


def temporal_attend(query, key_rows, value_rows):
    scores = jnp.einsum(
        "fphd,gphd->hpfg", query, key_rows, preferred_element_type=jnp.float32
    ) * HD ** (-0.5)
    weights = soft_weights(scores)
    result = jnp.einsum("hpfg,gphd->fphd", weights, value_rows, preferred_element_type=jnp.float32)
    return result.astype(jnp.bfloat16)


def per_device(queries, keys, values, text_keys, text_values, head_kinds, text_count, w_out):
    tok_rows = queries.shape[0]
    width = queries.shape[1]
    local_heads = width // HD
    group = lax.axis_index("head")
    kinds = lax.dynamic_slice_in_dim(head_kinds, group * local_heads, local_heads)
    text_k, text_v = (
        lax.all_gather(text_keys, "frame", axis=0, tiled=True),
        lax.all_gather(text_values, "frame", axis=0, tiled=True),
    )
    text_len = text_k.shape[0]
    query = queries.reshape(tok_rows, local_heads, HD)
    key_frame = keys.reshape(tok_rows, local_heads, HD)
    value_frame = values.reshape(tok_rows, local_heads, HD)
    stacked = (
        queries.reshape(1, tok_rows, local_heads, HD),
        keys.reshape(1, tok_rows, local_heads, HD),
        values.reshape(1, tok_rows, local_heads, HD),
    )
    moved_q, moved_k, moved_v = (
        lax.all_to_all(stacked[0], "frame", split_axis=1, concat_axis=0, tiled=True),
        lax.all_to_all(stacked[1], "frame", split_axis=1, concat_axis=0, tiled=True),
        lax.all_to_all(stacked[2], "frame", split_axis=1, concat_axis=0, tiled=True),
    )
    attended = temporal_attend(moved_q, moved_k, moved_v)
    returned = lax.all_to_all(attended, "frame", split_axis=0, concat_axis=1, tiled=True)
    temporal = returned.reshape(tok_rows, local_heads, HD)
    key_all = jnp.concatenate([key_frame, text_k.reshape(text_len, local_heads, HD)], axis=0)
    value_all = jnp.concatenate([value_frame, text_v.reshape(text_len, local_heads, HD)], axis=0)
    live = jnp.arange(tok_rows + text_len, dtype=jnp.int32) < tok_rows + text_count[0]
    spatial = spatial_attend(query, key_all, value_all, live)
    choose = (kinds == 1)[None, :, None]
    mixed = (
        jnp.where(choose, temporal.astype(jnp.float32), spatial)
        .astype(jnp.bfloat16)
        .reshape(tok_rows, width)
    )
    full_w = lax.all_gather(w_out, "frame", axis=1, tiled=True)
    return lax.psum_scatter(
        jnp.dot(mixed, full_w, preferred_element_type=jnp.float32).astype(jnp.bfloat16),
        "head",
        scatter_dimension=0,
        tiled=True,
    )


def solution(mesh):
    in_specs = (
        P("frame", "head"),
        P("frame", "head"),
        P("frame", "head"),
        P("frame", "head"),
        P("frame", "head"),
        P(),
        P(),
        P("head", "frame"),
    )
    out_specs = P(("frame", "head"), None)
    return jax.shard_map(
        per_device, mesh=mesh, in_specs=in_specs, out_specs=out_specs, check_vma=False
    )
```

profile of v0, /device:TPU:1, one launch (start us, length us, event | category | flops | bytes accessed | tf_op | source)
XLA Modules:
  0.0 207.4 jit_solution(7455302290442319795)
XLA Ops:
  6.5 0.0 copy-start
  6.5 0.0 all-gather.4.cloned.1.call-start
  6.5 0.7 all-gather.4.cloned.1.call-update
  7.3 1.1 copy.82
  8.3 0.9 copy.83
  9.2 11.6 %all-to-all-start = ((bf16[1,256,3,128]{3,2,0,1:T(4,128)(2,1)}), bf16[1,256,3,128]{3,2,0,1:T(4,128)(2,1)S(1)}, u32[]{:S(2)}, u32[]{:S(2)}) async-start(bf16[1,256,3,128]{3,2,0,1:T(4,128)(2,1)} %copy.83), calls=%async_computation | async-start | bytes 524288 | tf_op jit(solution)/shard_map/all_to_all | solution.py:53
  20.8 0.0 copy-start.1
  20.8 1.1 copy.85
  21.9 0.9 copy.86
  22.8 11.2 %all-to-all-done = bf16[1,256,3,128]{3,2,0,1:T(4,128)(2,1)S(1)} async-done(((bf16[1,256,3,128]{3,2,0,1:T(4,128)(2,1)}), bf16[1,256,3,128]{3,2,0,1:T(4,128)(2,1)S(1)}, u32[]{:S(2)}, u32[]{:S(2)}) %all-to-all-start) | async-done | bytes 196640 | tf_op jit(solution)/shard_map/all_to_all | solution.py:53
  34.0 4.7 %all-to-all-start.1 = ((bf16[1,256,3,128]{3,2,0,1:T(4,128)(2,1)}), bf16[1,256,3,128]{3,2,0,1:T(4,128)(2,1)S(1)}, u32[]{:S(2)}, u32[]{:S(2)}) async-start(bf16[1,256,3,128]{3,2,0,1:T(4,128)(2,1)} %copy.86), calls=%async_computation.1 | async-start | bytes 524288 | tf_op jit(solution)/shard_map/all_to_all | solution.py:54
  38.7 0.0 copy-done
  38.7 0.0 copy-start.2
  38.7 0.1 copy.90
  38.9 0.9 copy.91
  39.8 12.4 %all-to-all-done.1 = bf16[1,256,3,128]{3,2,0,1:T(4,128)(2,1)S(1)} async-done(((bf16[1,256,3,128]{3,2,0,1:T(4,128)(2,1)}), bf16[1,256,3,128]{3,2,0,1:T(4,128)(2,1)S(1)}, u32[]{:S(2)}, u32[]{:S(2)}) %all-to-all-start.1) | async-done | bytes 196640 | tf_op jit(solution)/shard_map/all_to_all | solution.py:54
  52.2 4.8 %all-to-all-start.2 = ((bf16[1,256,3,128]{3,2,0,1:T(4,128)(2,1)}), bf16[1,256,3,128]{3,2,0,1:T(4,128)(2,1)S(1)}, u32[]{:S(2)}, u32[]{:S(2)}) async-start(bf16[1,256,3,128]{3,2,0,1:T(4,128)(2,1)} %copy.91), calls=%async_computation.2 | async-start | bytes 524288 | tf_op jit(solution)/shard_map/all_to_all | solution.py:55
  57.0 0.2 copy.101
  57.2 0.0 copy-done.1
  57.2 40.9 %all-gather.1 = bf16[64,4,384]{2,1,0:T(4,128)(2,1)S(1)} all-gather(bf16[1,4,384]{2,1,0:T(4,128)(2,1)S(1)} %bitcast.50), channel_id=1, replica_groups=mesh['frame'=64,'head'=8] {'frame'}, dimensions={0}, use_global_device_ids=true | all-gather | bytes 199680 | tf_op jit(solution)/shard_map/all_gather | solution.py:40
  98.1 0.1 reshape.60
  98.9 0.0 copy-done.2
  98.9 36.9 %all-gather = bf16[64,4,384]{2,1,0:T(4,128)(2,1)S(1)} all-gather(bf16[1,4,384]{2,1,0:T(4,128)(2,1)S(1)} %bitcast.51), channel_id=1, replica_groups=mesh['frame'=64,'head'=8] {'frame'}, dimensions={0}, use_global_device_ids=true | all-gather | bytes 199680 | tf_op jit(solution)/shard_map/all_gather | solution.py:41
  135.8 0.1 reshape.58
  135.9 0.2 copy.99
  136.1 0.0 copy-start.3
  136.1 0.3 fusion.59
  136.4 0.0 all-to-all-done.2
  136.4 0.3 fusion.11
  136.7 0.8 copy.95
  137.5 7.5 %all-to-all-start.3 = ((bf16[64,4,3,128]{3,1,2,0:T(4,128)(2,1)}), bf16[64,4,3,128]{3,1,2,0:T(4,128)(2,1)S(1)}, u32[]{:S(2)}, u32[]{:S(2)}) async-start(bf16[64,4,3,128]{3,1,2,0:T(4,128)(2,1)} %copy.95), calls=%async_computation.3 | async-start | bytes 393216 | tf_op jit(solution)/shard_map/all_to_all | solution.py:58
  145.0 0.0 reduce-scatter.2.cloned.1.call-start
  145.1 0.0 copy-done.3
  145.1 0.1 dynamic-slice_compare_fusion
  145.1 0.6 fusion.64
  145.8 11.2 %all-to-all-done.3 = bf16[64,4,3,128]{3,1,2,0:T(4,128)(2,1)S(1)} async-done(((bf16[64,4,3,128]{3,1,2,0:T(4,128)(2,1)}), bf16[64,4,3,128]{3,1,2,0:T(4,128)(2,1)S(1)}, u32[]{:S(2)}, u32[]{:S(2)}) %all-to-all-start.3) | async-done | bytes 196640 | tf_op jit(solution)/shard_map/all_to_all | solution.py:58
  157.1 0.2 copy.97
  157.2 0.1 copy.106
  157.4 0.9 fusion.10
  158.3 0.0 all-gather.4.cloned.1.call-done
  158.3 3.8 %convolution_convert_fusion = bf16[256,3072]{1,0:T(8,128)(2,1)} fusion(bf16[256,384]{0,1:T(8,128)(2,1)S(1)} %bitcast.49, bf16[384,3072]{0,1:T(8,128)(2,1)} %all-gather.4.cloned.1.call-done), kind=kOutput, calls=%fused_computation.2 | convolution fusion | flops 604766208 | bytes 4128768 | tf_op jit(solution)/shard_map/dot_general | solution.py:72
  162.1 0.0 reduce-scatter.2.cloned.1.call-update
  162.2 38.4 %reduce-scatter.2.cloned.1.call-done = bf16[32,3072]{1,0:T(8,128)(2,1)} async-done(((bf16[256,3072]{1,0:T(8,128)(2,1)}), bf16[32,3072]{1,0:T(8,128)(2,1)}) %reduce-scatter.2.cloned.1.call-update) | async-done | bytes 196624 | tf_op jit(solution)/shard_map/reduce_scatter | solution.py:71
  (3 shorter events, 0.1 us)
Async XLA Ops:
  6.5 32.2 %copy-start = (bf16[256,384]{1,0:T(8,128)(2,1)S(1)}, bf16[256,384]{1,0:T(8,128)(2,1)}, u32[]{:S(2)}) copy-start(bf16[256,384]{1,0:T(8,128)(2,1)} %param.10) | copy-start | bytes 589828
  6.5 151.8 %all-gather.4.cloned.1.call-start = ((), (), s32[]{:S(2)}) async-start(), calls=%async_computation.5 | async-start | bytes 2396160 | tf_op jit(solution)/shard_map/all_gather | solution.py:70
  9.2 24.8 %all-to-all-start = ((bf16[1,256,3,128]{3,2,0,1:T(4,128)(2,1)}), bf16[1,256,3,128]{3,2,0,1:T(4,128)(2,1)S(1)}, u32[]{:S(2)}, u32[]{:S(2)}) async-start(bf16[1,256,3,128]{3,2,0,1:T(4,128)(2,1)} %copy.83), calls=%async_computation | async-start | bytes 524288 | tf_op jit(solution)/shard_map/all_to_all | solution.py:53
  20.8 36.3 %copy-start.1 = (bf16[4,384]{1,0:T(4,128)(2,1)S(1)}, bf16[4,384]{1,0:T(4,128)(2,1)}, u32[]{:S(2)}) copy-start(bf16[4,384]{1,0:T(4,128)(2,1)} %param.11) | copy-start | bytes 9220
  34.0 18.2 %all-to-all-start.1 = ((bf16[1,256,3,128]{3,2,0,1:T(4,128)(2,1)}), bf16[1,256,3,128]{3,2,0,1:T(4,128)(2,1)S(1)}, u32[]{:S(2)}, u32[]{:S(2)}) async-start(bf16[1,256,3,128]{3,2,0,1:T(4,128)(2,1)} %copy.86), calls=%async_computation.1 | async-start | bytes 524288 | tf_op jit(solution)/shard_map/all_to_all | solution.py:54
  38.7 60.1 %copy-start.2 = (bf16[4,384]{1,0:T(4,128)(2,1)S(1)}, bf16[4,384]{1,0:T(4,128)(2,1)}, u32[]{:S(2)}) copy-start(bf16[4,384]{1,0:T(4,128)(2,1)} %param.12) | copy-start | bytes 9220
  52.2 84.2 %all-to-all-start.2 = ((bf16[1,256,3,128]{3,2,0,1:T(4,128)(2,1)}), bf16[1,256,3,128]{3,2,0,1:T(4,128)(2,1)S(1)}, u32[]{:S(2)}, u32[]{:S(2)}) async-start(bf16[1,256,3,128]{3,2,0,1:T(4,128)(2,1)} %copy.91), calls=%async_computation.2 | async-start | bytes 524288 | tf_op jit(solution)/shard_map/all_to_all | solution.py:55
  136.1 9.0 %copy-start.3 = (s32[24]{0:T(128)S(1)}, s32[24]{0:T(128)}, u32[]{:S(2)}) copy-start(s32[24]{0:T(128)} %param.13) | copy-start | bytes 292
  137.5 19.5 %all-to-all-start.3 = ((bf16[64,4,3,128]{3,1,2,0:T(4,128)(2,1)}), bf16[64,4,3,128]{3,1,2,0:T(4,128)(2,1)S(1)}, u32[]{:S(2)}, u32[]{:S(2)}) async-start(bf16[64,4,3,128]{3,1,2,0:T(4,128)(2,1)} %copy.95), calls=%async_computation.3 | async-start | bytes 393216 | tf_op jit(solution)/shard_map/all_to_all | solution.py:58
  145.0 55.6 %reduce-scatter.2.cloned.1.call-start = ((), (), s32[]{:S(2)}) async-start(), calls=%async_computation.6 | async-start | bytes 1769472 | tf_op jit(solution)/shard_map/reduce_scatter | solution.py:71
Sparse Core Ops, SparseCore 0:
  10.6 88.8 all-gather.3
  162.3 38.2 reduce-scatter.1
where the time goes:
time: 211 us; the launch traced here: 207 us
  blocking collectives  77.8 us (37%)
  waiting for transfers between devices  74 us (35%)
  starting transfers between devices  28.7 us (14%)
  between operations  14.2 us (7%)
  local copies, waits for them, and re-layouts  6.62 us (3%)
  matrix products  5.95 us (3%)
    all_gather x1, blocking collectives, per_device(): lax.all_gather(text_keys, 'frame', axis=0, tiled=True)  40.9 us
    reduce_scatter x1, waiting for transfers between devices, per_device(): lax.psum_scatter(jnp.dot(mixed, full_w, preferred_element_type=jnp.float3...  38.4 us
    all_gather x1, blocking collectives, per_device(): lax.all_gather(text_values, 'frame', axis=0, tiled=True)  36.9 us
    all_to_all x1, waiting for transfers between devices, per_device(): lax.all_to_all(stacked[1], 'frame', split_axis=1, concat_axis=0, tiled=True)  12.4 us
    all_to_all x1, starting transfers between devices, per_device(): lax.all_to_all(stacked[0], 'frame', split_axis=1, concat_axis=0, tiled=True)  11.6 us
    all_to_all x1, waiting for transfers between devices, per_device(): lax.all_to_all(attended, 'frame', split_axis=0, concat_axis=1, tiled=True)  11.2 us
    all_to_all x1, waiting for transfers between devices, per_device(): lax.all_to_all(stacked[0], 'frame', split_axis=1, concat_axis=0, tiled=True)  11.2 us
    all_to_all x1, starting transfers between devices, per_device(): lax.all_to_all(attended, 'frame', split_axis=0, concat_axis=1, tiled=True)  7.49 us
  transfers between devices with their start and end apart: 6, of which 4 were waited for; matrix products, arithmetic and copies ran while one was open for 4% of the time, Pallas kernels for 0%

commit v1 on v0

v1 whole, which is shorter than its diff:
```python
import functools

import jax
import jax.numpy as jnp
from jax import lax
from jax.experimental import pallas as pl
from jax.experimental.pallas import tpu as pltpu
from jax.sharding import PartitionSpec as P

HD = 128
MESH = pl.DeviceIdType.MESH
F32 = jnp.float32
BF16 = jnp.bfloat16
NT = (((1,), (1,)), ((), ()))
NN = (((1,), (0,)), ((), ()))
SCALE = HD ** (-0.5)
FAR_FIRST = (4, 3, 5, 2, 6, 1, 7)


def dot(a, b, dims=NN):
    return lax.dot_general(a, b, dims, preferred_element_type=F32)


def send(src, dst, send_sem, recv_sem, **where):
    copy = pltpu.make_async_remote_copy(
        src_ref=src, dst_ref=dst, send_sem=send_sem, recv_sem=recv_sem,
        device_id=where, device_id_type=MESH,
    )
    copy.start()


def wait_for(ref, sem):
    pltpu.make_async_copy(ref, ref, sem).wait()


def swap_matrix():
    out = lax.broadcasted_iota(jnp.int32, (256, 256), 0)
    src = lax.broadcasted_iota(jnp.int32, (256, 256), 1)
    want = ((out // 4) % 8) * 32 + (out // 32) * 4 + out % 4
    return jnp.where(src == want, 1.0, 0.0).astype(BF16)


def text_matrix():
    out = lax.broadcasted_iota(jnp.int32, (64, 128), 0)
    src = lax.broadcasted_iota(jnp.int32, (64, 128), 1)
    want = ((out % 32) // 4) * 16 + (out // 32) * 4 + out % 4
    return jnp.where(src == want, 1.0, 0.0).astype(BF16)


def kernel(
    q_ref, k_ref, v_ref, slot_ref, kinds_ref, count_ref, out_ref,
    rx, sy, ty, oy, uy, sx, vx, wg, tk, tv, spat, mixed, part, rsend, rrecv,
    fx_s, fx_r, fy_s, fy_r, by_s, by_r, bx_s, bx_r,
    gy_s, gy_r, gx_s, gx_r, gp_s, gp_r, rs_s, rs_r,
):
    frame = lax.axis_index("frame")
    z = lax.axis_index("head")
    y = frame // 8
    j = frame % 8
    x = j // 2
    core = j % 2

    def at(yy, jj):
        return yy * 8 + jj

    def turn(base, step, size):
        return (base + step + size) % size

    j_right = turn(x, 1, 4) * 2 + core
    j_left = turn(x, -1, 4) * 2 + core
    j_far = turn(x, 2, 4) * 2 + core
    partner = at(y, x * 2 + 1 - core)

    barrier = pltpu.get_barrier_semaphore()
    for k in range(1, 8):
        pl.semaphore_signal(barrier, inc=1, device_id={"frame": at(turn(y, k, 8), j)}, device_id_type=MESH)
        pl.semaphore_signal(barrier, inc=1, device_id={"frame": at(y, turn(j, k, 8))}, device_id_type=MESH)
    for k in (1, -1):
        pl.semaphore_signal(barrier, inc=1, device_id={"head": turn(z, k, 8)}, device_id_type=MESH)
    pl.semaphore_wait(barrier, 16)

    def rows(block):
        return pl.ds(pl.multiple_of(block * 32, 32), 32)

    ins = (q_ref, k_ref, v_ref)
    for i in range(3):
        for k in FAR_FIRST:
            jj = turn(j, k, 8)
            send(ins[i].at[rows(jj)], rx.at[i, j], fx_s.at[i], fx_r.at[i], frame=at(y, jj))
        rx[i, j] = ins[i][rows(j), :]

    wg[y, j] = slot_ref[...]

    def gather_y(step):
        up = turn(y, 1 - step, 8)
        down = turn(y, step - 1, 8)
        cut_up = pl.ds(0, 32) if step == 4 else pl.ds(0, 64)
        cut_down = pl.ds(32, 32) if step == 4 else pl.ds(0, 64)
        src = wg.at[up, j, cut_up]
        send(src, src, gy_s.at[0, step - 1], gy_r.at[0, step - 1], frame=at(turn(y, 1, 8), j))
        src = wg.at[down, j, cut_down]
        send(src, src, gy_s.at[1, step - 1], gy_r.at[1, step - 1], frame=at(turn(y, -1, 8), j))

    def gathered_y(step):
        cut_up = pl.ds(0, 32) if step == 4 else pl.ds(0, 64)
        cut_down = pl.ds(32, 32) if step == 4 else pl.ds(0, 64)
        wait_for(wg.at[turn(y, -step, 8), j, cut_up], gy_r.at[0, step - 1])
        wait_for(wg.at[turn(y, step, 8), j, cut_down], gy_r.at[1, step - 1])

    gather_y(1)
    swap = swap_matrix()

    def turn_over(i):
        wait_for(rx.at[i, pl.ds(0, 7)], fx_r.at[i])
        sy[i] = dot(swap, rx[i].reshape(256, 384)).astype(BF16).reshape(8, 32, 384)
        for k in FAR_FIRST:
            yy = turn(y, k, 8)
            send(sy.at[i, yy], ty.at[i, y], fy_s.at[i], fy_r.at[i], frame=at(yy, j))
        ty[i, y] = sy[i, y]

    turn_over(0)
    gathered_y(1)
    gather_y(2)
    turn_over(1)
    gathered_y(2)
    gather_y(3)
    turn_over(2)
    gathered_y(3)
    gather_y(4)
    gathered_y(4)

    def block(jj):
        return wg.at[pl.ds(0, 8), jj]

    def low(jj):
        return wg.at[pl.ds(0, 4), jj]

    def high(jj):
        return wg.at[pl.ds(4, 4), jj]

    send(block(j), block(j), gx_s.at[0, 0], gx_r.at[0, 0], frame=at(y, j_right))
    send(block(j), block(j), gx_s.at[1, 0], gx_r.at[1, 0], frame=at(y, j_left))
    send(block(j), block(j), gp_s.at[0], gp_r.at[0], frame=partner)

    row = lax.broadcasted_iota(jnp.int32, (256, 256), 0)
    col = lax.broadcasted_iota(jnp.int32, (256, 256), 1)
    same = (row % 4) == (col % 4)
    for i in range(3):
        wait_for(ty.at[i, pl.ds(0, 7)], fy_r.at[i])
    for h in range(3):
        lanes = pl.ds(h * HD, HD)
        qh = ty[0, :, :, lanes].reshape(256, HD)
        kh = ty[1, :, :, lanes].reshape(256, HD)
        vh = ty[2, :, :, lanes].reshape(256, HD)
        scores = jnp.where(same, dot(qh, kh, NT) * SCALE, -1e30)
        expo = jnp.exp(scores - jnp.max(scores, axis=1, keepdims=True))
        total = jnp.sum(expo, axis=1, keepdims=True)
        oy[h] = (dot(expo.astype(BF16), vh) / total).astype(BF16).reshape(8, 32, HD)
        for k in FAR_FIRST:
            yy = turn(y, k, 8)
            send(oy.at[h, yy], uy.at[h, y], by_s.at[h], by_r.at[h], frame=at(yy, j))
        uy[h, y] = oy[h, y]

    wait_for(block(j_left), gx_r.at[0, 0])
    send(low(j_left), low(j_left), gx_s.at[0, 1], gx_r.at[0, 1], frame=at(y, j_right))
    send(block(j_left), block(j_left), gp_s.at[1], gp_r.at[1], frame=partner)
    wait_for(block(j_right), gx_r.at[1, 0])
    send(high(j_right), high(j_right), gx_s.at[1, 1], gx_r.at[1, 1], frame=at(y, j_left))
    send(block(j_right), block(j_right), gp_s.at[2], gp_r.at[2], frame=partner)
    wait_for(low(j_far), gx_r.at[0, 1])
    wait_for(high(j_far), gx_r.at[1, 1])
    send(block(j_far), block(j_far), gp_s.at[3], gp_r.at[3], frame=partner)

    for h in range(3):
        wait_for(uy.at[h, pl.ds(0, 7)], by_r.at[h])
        sx[h] = dot(swap, uy[h].reshape(256, HD)).astype(BF16).reshape(8, 32, HD)
        for k in FAR_FIRST:
            jj = turn(j, k, 8)
            send(sx.at[h, jj], vx.at[h, j], bx_s.at[h], bx_r.at[h], frame=at(y, jj))
        vx[h, j] = sx[h, j]

    shift = 1 - 2 * core
    for i, jj in enumerate((j, j_left, j_right, j_far)):
        wait_for(block(jj + shift), gp_r.at[i])

    pick = text_matrix()
    for b in range(8):
        both = dot(pick, wg[b, :, 48:64, :].reshape(128, 384)).astype(BF16)
        tk[b * 32:(b + 1) * 32, :] = both[:32]
        tv[b * 32:(b + 1) * 32, :] = both[32:]
    live = col < count_ref[0]
    for h in range(3):
        lanes = pl.ds(h * HD, HD)
        qh = q_ref[:, lanes]
        own = dot(qh, k_ref[:, lanes], NT) * SCALE
        text = jnp.where(live, dot(qh, tk[:, lanes], NT) * SCALE, -1e30)
        top = jnp.maximum(
            jnp.max(own, axis=1, keepdims=True), jnp.max(text, axis=1, keepdims=True)
        )
        e_own = jnp.exp(own - top)
        e_text = jnp.exp(text - top)
        total = jnp.sum(e_own, axis=1, keepdims=True) + jnp.sum(e_text, axis=1, keepdims=True)
        result = dot(e_own.astype(BF16), v_ref[:, lanes]) + dot(e_text.astype(BF16), tv[:, lanes])
        spat[:, lanes] = (result / total).astype(BF16)

    for h in range(3):
        lanes = pl.ds(h * HD, HD)
        wait_for(vx.at[h, pl.ds(0, 7)], bx_r.at[h])
        temporal = vx[h].reshape(256, HD)
        mixed[:, lanes] = jnp.where(kinds_ref[z * 3 + h] == 1, temporal, spat[:, lanes])

    ahead = turn(z, 1, 8)
    behind = turn(z, -1, 8)
    length = lambda b, way: 4 if (b + way) % 2 == 0 else 3

    def dest(b, way, stage):
        left = length(b, way) - stage
        return turn(z, left if way == 0 else -left, 8)

    def pass_on(src, b, way, stage):
        send(src, rrecv.at[way, b, stage], rs_s.at[way, b, stage], rs_r.at[way, b, stage],
             head=ahead if way == 0 else behind)

    for b in range(8):
        term = dot(mixed[...], wg[b, :, 0:48, :].reshape(384, 384), NT)
        part[b] = term.astype(BF16).reshape(8, 32, 384)
        for way in range(2):
            pass_on(part.at[b, dest(b, way, 0)], b, way, 0)
    for stage in range(1, 4):
        for b in range(8):
            for way in range(2):
                if stage < length(b, way):
                    wait_for(rrecv.at[way, b, stage - 1], rs_r.at[way, b, stage - 1])
                    own = part[b, dest(b, way, stage)].astype(F32)
                    rsend[way, b, stage] = (own + rrecv[way, b, stage - 1].astype(F32)).astype(BF16)
                    pass_on(rsend.at[way, b, stage], b, way, stage)
    for b in range(8):
        own = part[b, z].astype(F32)
        for way in range(2):
            last = length(b, way) - 1
            wait_for(rrecv.at[way, b, last], rs_r.at[way, b, last])
            own = own + rrecv[way, b, last].astype(F32)
        out_ref[:, b * 384:(b + 1) * 384] = own.astype(BF16)

    for i in range(3):
        wait_for(rx.at[i, pl.ds(0, 7)], fx_s.at[i])
        wait_for(sy.at[i, pl.ds(0, 7)], fy_s.at[i])
        wait_for(oy.at[i, pl.ds(0, 7)], by_s.at[i])
        wait_for(sx.at[i, pl.ds(0, 7)], bx_s.at[i])
    for way in range(2):
        for step in range(4):
            cut = pl.ds(0, 32) if step == 3 else pl.ds(0, 64)
            wait_for(wg.at[0, 0, cut], gy_s.at[way, step])
        wait_for(block(0), gx_s.at[way, 0])
        wait_for(low(0), gx_s.at[way, 1])
        for b in range(8):
            for stage in range(length(b, way)):
                wait_for(rsend.at[way, b, stage], rs_s.at[way, b, stage])
    for i in range(4):
        wait_for(block(0), gp_s.at[i])


def per_device(queries, keys, values, text_keys, text_values, head_kinds, text_count, w_out):
    slot = jnp.concatenate(
        [w_out.T, text_keys, text_values, jnp.zeros((8, w_out.shape[0]), BF16)], axis=0
    )
    vmem = pl.BlockSpec(memory_space=pltpu.VMEM)
    smem = pl.BlockSpec(memory_space=pltpu.SMEM)
    dma = pltpu.SemaphoreType.DMA
    return pl.pallas_call(
        kernel,
        out_shape=jax.ShapeDtypeStruct((32, 3072), BF16),
        in_specs=[vmem] * 4 + [smem] * 2,
        out_specs=vmem,
        scratch_shapes=[
            pltpu.VMEM((3, 8, 32, 384), BF16),
            pltpu.VMEM((3, 8, 32, 384), BF16),
            pltpu.VMEM((3, 8, 32, 384), BF16),
            pltpu.VMEM((3, 8, 32, HD), BF16),
            pltpu.VMEM((3, 8, 32, HD), BF16),
            pltpu.VMEM((3, 8, 32, HD), BF16),
            pltpu.VMEM((3, 8, 32, HD), BF16),
            pltpu.VMEM((8, 8, 64, 384), BF16),
            pltpu.VMEM((256, 384), BF16),
            pltpu.VMEM((256, 384), BF16),
            pltpu.VMEM((256, 384), BF16),
            pltpu.VMEM((256, 384), BF16),
            pltpu.VMEM((8, 8, 32, 384), BF16),
            pltpu.VMEM((2, 8, 4, 32, 384), BF16),
            pltpu.VMEM((2, 8, 4, 32, 384), BF16),
        ]
        + [dma((3,))] * 8
        + [dma((2, 4))] * 2
        + [dma((2, 2))] * 2
        + [dma((4,))] * 2
        + [dma((2, 8, 4))] * 2,
        compiler_params=pltpu.CompilerParams(
            collective_id=0, has_side_effects=True, vmem_limit_bytes=40 * 1024 * 1024
        ),
    )(queries, keys, values, slot, head_kinds, text_count)


def solution(mesh):
    in_specs = (
        P("frame", "head"),
        P("frame", "head"),
        P("frame", "head"),
        P("frame", "head"),
        P("frame", "head"),
        P(),
        P(),
        P("head", "frame"),
    )
    out_specs = P(("frame", "head"), None)
    return jax.shard_map(
        per_device, mesh=mesh, in_specs=in_specs, out_specs=out_specs, check_vma=False
    )
```

time: 211 us -> 84.5 us (0.40); the launches traced: 207 us -> 84.2 us
  Pallas kernels: 0 us -> 78.5 us
  blocking collectives: 77.8 us -> 0 us
  waiting for transfers between devices: 74 us -> 0 us
  starting transfers between devices: 28.7 us -> 0 us
  between operations: 14.2 us -> 0.72 us
  matrix products: 5.95 us -> 0 us
  local copies, waits for them, and re-layouts: 6.62 us -> 4.13 us
    pallas_call x0 -> x1, Pallas kernels: none -> 78.5 us  [per_device(): pl.pallas_call(kernel, out_shape=jax.ShapeDtypeStruct((32, 3072), BF16),...]
    all_gather x2 -> x0, blocking collectives: 77.8 us -> none  [the longest x1 40.9 us: per_device(): lax.all_gather(text_keys, 'frame', axis=0, tiled=True)]
    reduce_scatter x1 -> x0, waiting for transfers between devices: 38.4 us -> none  [per_device(): lax.psum_scatter(jnp.dot(mixed, full_w, preferred_element_type=jnp.float3...]
    all_to_all x4 -> x0, waiting for transfers between devices: 34.8 us -> none  [the longest x1 12.4 us: per_device(): lax.all_to_all(stacked[1], 'frame', split_axis=1, concat_axis=0, tiled=True)]
    all_to_all x4 -> x0, starting transfers between devices: 28.7 us -> none  [the longest x1 11.6 us: per_device(): lax.all_to_all(stacked[0], 'frame', split_axis=1, concat_axis=0, tiled=True)]
    dot_general x3 -> x0, matrix products: 5 us -> none  [the longest x1 3.85 us: per_device(): jnp.dot(mixed, full_w, preferred_element_type=jnp.float32)]
    reshape x8 -> x0, local copies, waits for them, and re-layouts: 3.16 us -> none  [the longest x1 0.88 us: per_device(): queries.reshape(1, tok_rows, local_heads, HD)]
  transfers between devices with their start and end apart: 6 -> 0, of which waited for: 4 -> 0; matrix products, arithmetic and copies ran while one was open for 4% -> 0% of each run, Pallas kernels for 0% -> 0%
where the time goes in v1:
time: 84.5 us; the launch traced here: 84.2 us
  Pallas kernels  78.5 us (93%)
  local copies, waits for them, and re-layouts  4.13 us (5%)
  other arithmetic  0.86 us (1%)
    pallas_call x1, Pallas kernels, per_device(): pl.pallas_call(kernel, out_shape=jax.ShapeDtypeStruct((32, 3072), BF16),...  78.5 us
    unnamed x13, local copies, waits for them, and re-layouts  4.05 us

profile of v1, /device:TPU:1, one launch (start us, length us, event | category | flops | bytes accessed | tf_op | source)
XLA Modules:
  0.0 84.2 jit_solution(3228028510863265181)
XLA Ops:
  0.0 0.0 copy-start.5
  0.7 0.0 copy-start.4
  0.7 0.1 pad.3.clone
  0.8 0.0 copy-done.5
  0.8 0.6 copy-done.4
  1.4 0.0 copy-start.3
  1.4 0.9 %maximum_maximum_fusion.slot_ref = bf16[64,384]{1,0:T(8,128)(2,1)S(1)} fusion(bf16[4,384]{1,0:T(4,128)(2,1)S(1)} %copy-done.4, bf16[4,384]{1,0:T(4,128)(2,1)S(1)} %copy-done.5, bf16[48,384]{1,0:T(8,128)(2,1)} %bitcast.1, bf16[64]{0:T(256)(128)(2,1)S(1)} %pad.3.clone), kind=kLoop, calls=%fused_computation | loop fusion | flops 196608 | bytes 92288 | tf_op jit(solution)/shard_map/concatenate | solution.py:264
  2.2 0.0 copy-done.3
  2.2 0.0 copy-start
  2.2 0.9 %copy-done = bf16[256,384]{1,0:T(8,128)(2,1)S(1)} copy-done((bf16[256,384]{1,0:T(8,128)(2,1)S(1)}, bf16[256,384]{1,0:T(8,128)(2,1)}, u32[]{:S(2)}) %copy-start) | copy-done | bytes 196632
  3.2 0.0 copy-start.1
  3.2 0.9 %copy-done.1 = bf16[256,384]{1,0:T(8,128)(2,1)S(1)} copy-done((bf16[256,384]{1,0:T(8,128)(2,1)S(1)}, bf16[256,384]{1,0:T(8,128)(2,1)}, u32[]{:S(2)}) %copy-start.1) | copy-done | bytes 196632
  4.1 0.0 copy-start.2
  4.1 0.9 %copy-done.2 = bf16[256,384]{1,0:T(8,128)(2,1)S(1)} copy-done((bf16[256,384]{1,0:T(8,128)(2,1)S(1)}, bf16[256,384]{1,0:T(8,128)(2,1)}, u32[]{:S(2)}) %copy-start.2) | copy-done | bytes 196632
  5.0 78.5 %shard_map.82 = bf16[32,3072]{1,0:T(8,128)(2,1)S(1)} custom-call(bf16[256,384]{1,0:T(8,128)(2,1)S(1)} %copy-done, bf16[256,384]{1,0:T(8,128)(2,1)S(1)} %copy-done.1, bf16[256,384]{1,0:T(8,128)(2,1)S(1)} %copy-done.2, bf16[64,384]{1,0:T(8,128)(2,1)S(1)} %maximum_maximum_fusion.slot_ref, s32[24]{0:T(128)S(1)} %copy-done.3, s32[1]{0:T(128)S(6)} %copy.10.count_ref), custom_call_target="tpu_custom_call" | custom-call | tf_op jit(solution)/shard_map/pallas_call | solution.py:270
  83.5 0.7 copy.11
  (1 shorter events, 0.0 us)
Async XLA Ops:
  0.0 0.8 copy-start.5
  0.7 0.7 copy-start.4
  1.4 0.9 %copy-start.3 = (s32[24]{0:T(128)S(1)}, s32[24]{0:T(128)}, u32[]{:S(2)}) copy-start(s32[24]{0:T(128)} %kinds_ref.1) | copy-start | bytes 292
  2.2 0.9 %copy-start = (bf16[256,384]{1,0:T(8,128)(2,1)S(1)}, bf16[256,384]{1,0:T(8,128)(2,1)}, u32[]{:S(2)}) copy-start(bf16[256,384]{1,0:T(8,128)(2,1)} %q_ref.1) | copy-start | bytes 589828
  3.2 0.9 %copy-start.1 = (bf16[256,384]{1,0:T(8,128)(2,1)S(1)}, bf16[256,384]{1,0:T(8,128)(2,1)}, u32[]{:S(2)}) copy-start(bf16[256,384]{1,0:T(8,128)(2,1)} %k_ref.1) | copy-start | bytes 589828
  4.1 0.9 %copy-start.2 = (bf16[256,384]{1,0:T(8,128)(2,1)S(1)}, bf16[256,384]{1,0:T(8,128)(2,1)}, u32[]{:S(2)}) copy-start(bf16[256,384]{1,0:T(8,128)(2,1)} %v_ref.1) | copy-start | bytes 589828

commit v2 on v0

v2 whole, which is shorter than its diff:
```python
import jax
import jax.numpy as jnp
from jax import lax
from jax.experimental import pallas as pl
from jax.experimental.pallas import tpu as pltpu
from jax.sharding import PartitionSpec as P

HD = 128
MESH = pl.DeviceIdType.MESH
F32 = jnp.float32
BF16 = jnp.bfloat16
NT = (((1,), (1,)), ((), ()))
NN = (((1,), (0,)), ((), ()))
SCALE = HD ** (-0.5)
DY = (0, 1, 2, 3, 6, 7, 4, 5)
GROUPS = ((0, 1), (1, 5), (6, 2))
FAR_FIRST = (4, 3, 5, 2, 6, 1, 7)


def dot(a, b, dims=NN):
    return lax.dot_general(a, b, dims, preferred_element_type=F32)


def send(src, dst, send_sem, recv_sem, **where):
    copy = pltpu.make_async_remote_copy(
        src_ref=src, dst_ref=dst, send_sem=send_sem, recv_sem=recv_sem,
        device_id=where, device_id_type=MESH,
    )
    copy.start()


def wait_for(ref, sem):
    pltpu.make_async_copy(ref, ref, sem).wait()


def one_hot(rows, cols, want):
    out = lax.broadcasted_iota(jnp.int32, (rows, cols), 0)
    src = lax.broadcasted_iota(jnp.int32, (rows, cols), 1)
    return jnp.where(src == want(out), 1.0, 0.0).astype(BF16)


def kernel(
    q_hbm, k_hbm, v_hbm, tk_hbm, tv_hbm, w_hbm, kinds_ref, count_ref, out_ref,
    qb, kb, vb, tkb, tvb, pack, got, turned, done, back, backed, wg, text32, text, toks, spat, mixed,
    part, rsend, rrecv,
    in_sem, f_s, f_r, b_s, b_r, ty_s, ty_r, tx_s, tx_r, tp_s, tp_r,
    wy_s, wy_r, wz_s, wz_r, wx_s, wx_r, wf_s, wf_r, wp_s, wp_r, rs_s, rs_r,
):
    frame = lax.axis_index("frame")
    z = lax.axis_index("head")
    y = frame // 8
    j = frame % 8
    x = j // 2
    core = j % 2

    def at(yy, jj):
        return yy * 8 + jj

    def turn(base, step, size):
        return (base + step + size) % size

    j_right = turn(x, 1, 4) * 2 + core
    j_left = turn(x, -1, 4) * 2 + core
    j_far = turn(x, 2, 4) * 2 + core
    shift = 1 - 2 * core
    partner = at(y, j + shift)

    barrier = pltpu.get_barrier_semaphore()

    def greet(i, carry):
        pl.semaphore_signal(barrier, inc=1, device_id={"frame": (frame + i) % 64}, device_id_type=MESH)
        return carry

    lax.fori_loop(1, 64, greet, 0)
    for k in (1, -1):
        pl.semaphore_signal(barrier, inc=1, device_id={"head": turn(z, k, 8)}, device_id_type=MESH)

    loads = [
        pltpu.make_async_copy(src, dst, in_sem.at[i])
        for i, (src, dst) in enumerate(
            ((q_hbm, qb), (k_hbm, kb), (v_hbm, vb), (tk_hbm, tkb), (tv_hbm, tvb), (w_hbm, wg.at[0, j]))
        )
    ]
    for load in loads:
        load.start()
    text32[...] = jnp.zeros_like(text32)
    loads[3].wait()
    loads[4].wait()
    for h in range(3):
        lanes = pl.ds(h * HD, HD)
        text32[h * 4:h * 4 + 4, :] = tkb[:, lanes].astype(F32)
        text32[12 + h * 4:16 + h * 4, :] = tvb[:, lanes].astype(F32)
    text[0, j] = text32[...].astype(BF16)
    for i, (load, buf) in enumerate(zip(loads, (qb, kb, vb))):
        load.wait()
        for h in range(3):
            units = buf[:, h * HD:(h + 1) * HD].reshape(8, 2, 16, HD)
            for half in range(2):
                pack[half, :, h, i * 16:(i + 1) * 16, :] = units[:, half]

    loads[5].wait()

    def unit_j(half, k):
        return 2 * k if half == 0 else (2 * k + 4) % 8 + 1

    active = [(j % 2) == 0, (j % 2) == 1]
    active = [
        jnp.logical_or(jnp.logical_or(j == unit_j(half, 0), j == unit_j(half, 1)), j == unit_j(half, 2))
        for half in range(2)
    ]
    my_k = [j // 2, ((j + 3) % 8) // 2]

    pl.semaphore_wait(barrier, 65)

    def text_y():
        for d in FAR_FIRST:
            send(text.at[0, j], text.at[d, j], ty_s.at[d], ty_r.at[d], frame=at(turn(y, -d, 8), j))

    def text_x():
        for d in range(1, 8):
            wait_for(text.at[d, j], ty_r.at[d])
        col = text.at[pl.ds(0, 8), j]
        for i, jj in enumerate((j_far, j_right, j_left)):
            send(col, col, tx_s.at[i], tx_r.at[i], frame=at(y, jj))
        send(col, col, tp_s.at[3], tp_r.at[3], frame=partner)

    def text_p():
        for i, jj in enumerate((j_far, j_left, j_right)):
            col = text.at[pl.ds(0, 8), jj]
            wait_for(col, tx_r.at[i])
            send(col, col, tp_s.at[i], tp_r.at[i], frame=partner)

    def text_done():
        for i, jj in enumerate((j_far, j_left, j_right, j)):
            wait_for(text.at[pl.ds(0, 8), jj + shift], tp_r.at[i])

    def forward(half):
        def one(i, carry):
            yy = (y + i) % 8
            for k in range(3):
                jj = unit_j(half, k)

                @pl.when(at(yy, jj) != frame)
                def _():
                    send(pack.at[half, yy, k], got.at[frame], f_s.at[half], f_r, frame=at(yy, jj))

            return carry

        lax.fori_loop(1, 9, one, 0)

        @pl.when(active[half])
        def _():
            got[frame] = pack[half, y, my_k[half]]

    def counted(half, ref, sem):
        @pl.when(active[half])
        def _():
            wait_for(ref.at[pl.ds(0, 23)], sem)

        @pl.when(jnp.logical_not(active[half]))
        def _():
            wait_for(ref.at[pl.ds(0, 24)], sem)

    def forward_sent(half):
        counted(half, got, f_s.at[half])

    def temporal(half):
        @pl.when(active[half])
        def _():
            wait_for(got.at[pl.ds(0, 63)], f_r)
            swap = one_hot(256, 256, lambda out: (out % 16) * 16 + out // 16)
            for c in range(4):
                rows = jnp.concatenate(
                    [got[c * 16:(c + 1) * 16, i * 16:(i + 1) * 16, :].reshape(256, HD) for i in range(3)],
                    axis=1,
                )
                rows = dot(swap, rows).astype(BF16)
                for i in range(3):
                    turned[i, :, c * 16:(c + 1) * 16, :] = rows[:, i * HD:(i + 1) * HD].reshape(16, 16, HD)
            row = lax.broadcasted_iota(jnp.int32, (256, 256), 0)
            col = lax.broadcasted_iota(jnp.int32, (256, 256), 1)
            same = (row // 64) == (col // 64)
            for g in range(4):
                qg, kg, vg = [turned[i, g * 4:(g + 1) * 4].reshape(256, HD) for i in range(3)]
                scores = jnp.where(same, dot(qg, kg, NT) * SCALE, -1e30)
                expo = jnp.exp(scores - jnp.max(scores, axis=1, keepdims=True))
                total = jnp.sum(expo, axis=1, keepdims=True)
                result = dot(expo.astype(BF16), vg) / total
                done[g * 4:(g + 1) * 4] = result.astype(BF16).reshape(4, 64, HD)
            for c in range(4):
                rows = dot(swap, done[:, c * 16:(c + 1) * 16, :].reshape(256, HD))
                back[c * 16:(c + 1) * 16] = rows.astype(BF16).reshape(16, 16, HD)

            def one(i, carry):
                to = (frame + i) % 64
                send(back.at[to], backed.at[half, y * 3 + my_k[half]], b_s, b_r.at[half], frame=to)
                return carry

            lax.fori_loop(1, 64, one, 0)
            backed[half, y * 3 + my_k[half]] = back[frame]

    def w_y1():
        for i, d in ((3, 3), (2, 2), (1, 1), (4, 6), (5, 7)):
            send(wg.at[0, j], wg.at[i, j], wy_s.at[i], wy_r.at[i], frame=at(turn(y, -d, 8), j))

    def w_y2():
        for i in range(1, 6):
            wait_for(wg.at[i, j], wy_r.at[i])
        for i, d in ((7, 2), (6, 1)):
            send(wg.at[3, j], wg.at[i, j], wz_s.at[i - 6], wz_r.at[i - 6], frame=at(turn(y, -d, 8), j))

    def w_y3():
        for i in (6, 7):
            wait_for(wg.at[i, j], wz_r.at[i - 6])

    def cut(group, jj):
        first, count = GROUPS[group]
        return wg.at[pl.ds(first, count), jj]

    def w_x1(group):
        src = cut(group, j)
        send(src, src, wx_s.at[0, group], wx_r.at[0, group], frame=at(y, j_right))
        send(src, src, wx_s.at[1, group], wx_r.at[1, group], frame=at(y, j_left))
        send(src, src, wp_s.at[0, group], wp_r.at[0, group], frame=partner)

    def w_x2(group):
        src = cut(group, j_right)
        wait_for(src, wx_r.at[1, group])
        send(src, src, wf_s.at[group], wf_r.at[group], frame=at(y, j_left))
        send(src, src, wp_s.at[1, group], wp_r.at[1, group], frame=partner)
        src = cut(group, j_left)
        wait_for(src, wx_r.at[0, group])
        send(src, src, wp_s.at[2, group], wp_r.at[2, group], frame=partner)

    def w_x3(group):
        src = cut(group, j_far)
        wait_for(src, wf_r.at[group])
        send(src, src, wp_s.at[3, group], wp_r.at[3, group], frame=partner)

    def w_done(group):
        for i, jj in enumerate((j, j_right, j_left, j_far)):
            wait_for(cut(group, jj + shift), wp_r.at[i, group])

    def spatial():
        pick = one_hot(192, 256, lambda out: ((out % 32) // 4) * 32 + (out // 32) * 4 + out % 4)
        for d in range(8):
            rows = dot(pick, text[d].reshape(256, HD)).astype(BF16)
            toks[:, d * 32:(d + 1) * 32, :] = rows.reshape(6, 32, HD)
        col = lax.broadcasted_iota(jnp.int32, (256, 256), 1)
        live = (y * 32 + col) % 256 < count_ref[0]
        for h in range(3):
            lanes = pl.ds(h * HD, HD)
            qh = qb[:, lanes]
            own = dot(qh, kb[:, lanes], NT) * SCALE
            other = jnp.where(live, dot(qh, toks[h], NT) * SCALE, -1e30)
            top = jnp.maximum(
                jnp.max(own, axis=1, keepdims=True), jnp.max(other, axis=1, keepdims=True)
            )
            e_own = jnp.exp(own - top)
            e_other = jnp.exp(other - top)
            total = jnp.sum(e_own, axis=1, keepdims=True) + jnp.sum(e_other, axis=1, keepdims=True)
            result = dot(e_own.astype(BF16), vb[:, lanes]) + dot(e_other.astype(BF16), toks[3 + h])
            spat[:, :, :, lanes] = (result / total).astype(BF16).reshape(8, 2, 16, HD)

    def length(pair, way):
        return 4 if (pair + way) % 2 == 0 else 3

    def dest(pair, way, stage):
        left = length(pair, way) - stage
        return turn(z, left if way == 0 else -left, 8)

    def pass_on(src, half, pair, way, stage):
        at_sem = (half, way, pair, stage)
        send(src, rrecv.at[at_sem], rs_s.at[at_sem], rs_r.at[at_sem], head=turn(z, 1 - 2 * way, 8))

    def mix(half):
        counted(half, backed.at[half], b_r.at[half])
        for h in range(3):
            lanes = pl.ds(h * HD, HD)
            temp = backed[half].reshape(8, 3, 16, HD)[:, h].reshape(128, HD)
            own = spat[:, half, :, lanes].reshape(128, HD)
            mixed[half, :, lanes] = jnp.where(kinds_ref[z * 3 + h] == 1, temp, own)

    def project(half, pair):
        for i in range(2):
            term = dot(mixed[half], wg[pair * 2 + i].reshape(384, 384), NT)
            part[half, pair, :, i] = term.astype(BF16).reshape(8, 16, 384)
        for way in range(2):
            pass_on(part.at[half, pair, dest(pair, way, 0)], half, pair, way, 0)

    def reduce(half, stage):
        for pair in range(4):
            for way in range(2):
                if stage < length(pair, way):
                    before = (half, way, pair, stage - 1)
                    now = (half, way, pair, stage)
                    wait_for(rrecv.at[before], rs_r.at[before])
                    own = part[half, pair, dest(pair, way, stage)].astype(F32)
                    rsend[now] = (own + rrecv[before].astype(F32)).astype(BF16)
                    pass_on(rsend.at[now], half, pair, way, stage)

    def finish(half):
        for pair in range(4):
            own = part[half, pair, z].astype(F32)
            for way in range(2):
                last = (half, way, pair, length(pair, way) - 1)
                wait_for(rrecv.at[last], rs_r.at[last])
                own = own + rrecv[last].astype(F32)
            for i in range(2):
                block = turn(y, DY[pair * 2 + i], 8)
                columns = pl.ds(pl.multiple_of(block * 384, 384), 384)
                out_ref[half * 16:(half + 1) * 16, columns] = own[i].astype(BF16)

    def drain_rs(half):
        for pair in range(4):
            for way in range(2):
                for stage in range(length(pair, way)):
                    now = (half, way, pair, stage)
                    wait_for(rrecv.at[now], rs_s.at[now])

    def drain_text():
        for d in range(1, 8):
            wait_for(text.at[d, j], ty_s.at[d])
        col = text.at[pl.ds(0, 8), j]
        for i in range(3):
            wait_for(col, tx_s.at[i])
        for i in range(4):
            wait_for(col, tp_s.at[i])

    def drain_w():
        for i in range(1, 6):
            wait_for(wg.at[i, j], wy_s.at[i])
        for i in range(2):
            wait_for(wg.at[i, j], wz_s.at[i])
        for group in range(3):
            wait_for(cut(group, j), wx_s.at[0, group])
            wait_for(cut(group, j), wx_s.at[1, group])
            wait_for(cut(group, j), wf_s.at[group])
            for i in range(4):
                wait_for(cut(group, j), wp_s.at[i, group])

    def drain_back():
        @pl.when(jnp.logical_or(active[0], active[1]))
        def _():
            wait_for(back.at[pl.ds(0, 63)], b_s)

    w_y1()
    w_x1(0)
    text_y()
    forward(0)
    w_y2()
    w_x1(1)
    w_x2(0)
    text_x()
    forward_sent(0)
    forward(1)
    w_y3()
    w_x1(2)
    w_x2(1)
    w_x3(0)
    temporal(0)
    text_p()
    text_done()
    spatial()
    w_x2(2)
    w_x3(1)
    w_x3(2)
    w_done(0)
    w_done(1)
    w_done(2)
    mix(0)
    project(0, 0)
    project(0, 1)
    project(0, 2)
    project(0, 3)
    temporal(1)
    reduce(0, 1)
    reduce(0, 2)
    mix(1)
    project(1, 0)
    project(1, 1)
    project(1, 2)
    project(1, 3)
    reduce(0, 3)
    reduce(1, 1)
    reduce(1, 2)
    reduce(1, 3)
    finish(0)
    finish(1)
    forward_sent(1)
    drain_rs(0)
    drain_rs(1)
    drain_text()
    drain_w()
    drain_back()


def per_device(queries, keys, values, text_keys, text_values, head_kinds, text_count, w_out):
    anywhere = pl.BlockSpec(memory_space=pl.ANY)
    vmem = pl.BlockSpec(memory_space=pltpu.VMEM)
    smem = pl.BlockSpec(memory_space=pltpu.SMEM)
    dma = pltpu.SemaphoreType.DMA
    return pl.pallas_call(
        kernel,
        out_shape=jax.ShapeDtypeStruct((32, 3072), BF16),
        in_specs=[anywhere] * 6 + [smem] * 2,
        out_specs=vmem,
        scratch_shapes=[
            pltpu.VMEM((256, 384), BF16),
            pltpu.VMEM((256, 384), BF16),
            pltpu.VMEM((256, 384), BF16),
            pltpu.VMEM((4, 384), BF16),
            pltpu.VMEM((4, 384), BF16),
            pltpu.VMEM((2, 8, 3, 48, HD), BF16),
            pltpu.VMEM((64, 48, HD), BF16),
            pltpu.VMEM((3, 16, 64, HD), BF16),
            pltpu.VMEM((16, 64, HD), BF16),
            pltpu.VMEM((64, 16, HD), BF16),
            pltpu.VMEM((2, 24, 16, HD), BF16),
            pltpu.VMEM((8, 8, 48, 384), BF16),
            pltpu.VMEM((32, HD), F32),
            pltpu.VMEM((8, 8, 32, HD), BF16),
            pltpu.VMEM((6, 256, HD), BF16),
            pltpu.VMEM((8, 2, 16, 384), BF16),
            pltpu.VMEM((2, 128, 384), BF16),
            pltpu.VMEM((2, 4, 8, 2, 16, 384), BF16),
            pltpu.VMEM((2, 2, 4, 4, 2, 16, 384), BF16),
            pltpu.VMEM((2, 2, 4, 4, 2, 16, 384), BF16),
            dma((6,)),
            dma((2,)),
            dma,
            dma,
            dma((2,)),
            dma((8,)),
            dma((8,)),
            dma((3,)),
            dma((3,)),
            dma((4,)),
            dma((4,)),
            dma((6,)),
            dma((6,)),
            dma((2,)),
            dma((2,)),
            dma((2, 3)),
            dma((2, 3)),
            dma((3,)),
            dma((3,)),
            dma((4, 3)),
            dma((4, 3)),
            dma((2, 2, 4, 4)),
            dma((2, 2, 4, 4)),
        ],
        compiler_params=pltpu.CompilerParams(
            collective_id=0, has_side_effects=True, vmem_limit_bytes=60 * 1024 * 1024
        ),
    )(queries, keys, values, text_keys, text_values, w_out.T, head_kinds, text_count)


def solution(mesh):
    in_specs = (
        P("frame", "head"),
        P("frame", "head"),
        P("frame", "head"),
        P("frame", "head"),
        P("frame", "head"),
        P(),
        P(),
        P("head", "frame"),
    )
    out_specs = P(("frame", "head"), None)
    return jax.shard_map(
        per_device, mesh=mesh, in_specs=in_specs, out_specs=out_specs, check_vma=False
    )
```

time: 211 us -> 77.6 us (0.37)
  the two profiles are of different devices: /device:TPU:1 before, /device:TPU:16 now
where the time goes in v2:
time: 77.6 us; the launch traced here: 77.4 us
  Pallas kernels  75.2 us (97%)
  local copies, waits for them, and re-layouts  1.62 us (2%)
    pallas_call x1, Pallas kernels, per_device(): pl.pallas_call(kernel, out_shape=jax.ShapeDtypeStruct((32, 3072), BF16),...  75.2 us
    unnamed x1, local copies, waits for them, and re-layouts  1.62 us

profile of v2, /device:TPU:16, one launch (start us, length us, event | category | flops | bytes accessed | tf_op | source)
XLA Modules:
  0.0 77.4 jit_solution(16737580025705213077)
XLA Ops:
  0.7 75.2 %shard_map.82 = bf16[32,3072]{1,0:T(8,128)(2,1)} custom-call(bf16[256,384]{1,0:T(8,128)(2,1)} %q_hbm.1, bf16[256,384]{1,0:T(8,128)(2,1)} %k_hbm.1, bf16[256,384]{1,0:T(8,128)(2,1)} %v_hbm.1, bf16[4,384]{1,0:T(4,128)(2,1)} %tk_hbm.1, bf16[4,384]{1,0:T(4,128)(2,1)} %tv_hbm.1, bf16[48,384]{1,0:T(8,128)(2,1)} %bitcast.1, s32[24]{0:T(128)} %kinds_ref.1, ...), custom_call_target="tpu_custom_call" | custom-call | tf_op jit(solution)/shard_map/pallas_call | solution.py:403
  75.8 1.6 %copy.11 = bf16[32,3072]{1,0:T(8,128)(2,1)} copy(bf16[32,3072]{1,0:T(8,128)(2,1)} %shard_map.82) | data formatting | bytes 393216

commit v3 on v2

--- a/solution.py
+++ b/solution.py
@@ -12,8 +12,10 @@
 NT = (((1,), (1,)), ((), ()))
 NN = (((1,), (0,)), ((), ()))
 SCALE = HD ** (-0.5)
-DY = (0, 1, 2, 3, 6, 7, 4, 5)
-GROUPS = ((0, 1), (1, 5), (6, 2))
+DY = (0, 1, 7, 2, 6, 3, 4, 5)
+BATCHES = ((4, 7), (3, 6), (2, 5), (1, 0))
+GROUPS = ((0, 1), (1, 2), (3, 2), (5, 1), (6, 2))
+ONWARD = (1, 0, 1, 0, 1)
 FAR_FIRST = (4, 3, 5, 2, 6, 1, 7)
 
 
@@ -44,7 +46,7 @@
     qb, kb, vb, tkb, tvb, pack, got, turned, done, back, backed, wg, text32, text, toks, spat, mixed,
     part, rsend, rrecv,
     in_sem, f_s, f_r, b_s, b_r, ty_s, ty_r, tx_s, tx_r, tp_s, tp_r,
-    wy_s, wy_r, wz_s, wz_r, wx_s, wx_r, wf_s, wf_r, wp_s, wp_r, rs_s, rs_r,
+    wy_s, wy_r, wx_s, wx_r, wf_s, wf_r, wp_s, wp_r, rs_s, rs_r,
 ):
     frame = lax.axis_index("frame")
     z = lax.axis_index("head")
@@ -100,15 +102,11 @@
 
     loads[5].wait()
 
-    def unit_j(half, k):
-        return 2 * k if half == 0 else (2 * k + 4) % 8 + 1
-
-    active = [(j % 2) == 0, (j % 2) == 1]
-    active = [
-        jnp.logical_or(jnp.logical_or(j == unit_j(half, 0), j == unit_j(half, 1)), j == unit_j(half, 2))
-        for half in range(2)
-    ]
-    my_k = [j // 2, ((j + 3) % 8) // 2]
+    def unit_j(half, yy, k):
+        return ((yy + k) % 4) * 2 + half
+
+    my_k = (x - y + 8) % 4
+    active = [jnp.logical_and(core == half, my_k < 3) for half in range(2)]
 
     pl.semaphore_wait(barrier, 65)
 
@@ -120,49 +118,60 @@
         for d in range(1, 8):
             wait_for(text.at[d, j], ty_r.at[d])
         col = text.at[pl.ds(0, 8), j]
-        for i, jj in enumerate((j_far, j_right, j_left)):
-            send(col, col, tx_s.at[i], tx_r.at[i], frame=at(y, jj))
+        send(col, col, tx_s.at[0], tx_r.at[0], frame=at(y, j_left))
+        send(col, col, tx_s.at[1], tx_r.at[1], frame=at(y, j_right))
         send(col, col, tp_s.at[3], tp_r.at[3], frame=partner)
 
+    def text_x2():
+        col = text.at[pl.ds(0, 8), j_right]
+        wait_for(col, tx_r.at[0])
+        send(col, col, tx_s.at[2], tx_r.at[2], frame=at(y, j_left))
+        send(col, col, tp_s.at[2], tp_r.at[2], frame=partner)
+        col = text.at[pl.ds(0, 8), j_left]
+        wait_for(col, tx_r.at[1])
+        send(col, col, tp_s.at[1], tp_r.at[1], frame=partner)
+
     def text_p():
-        for i, jj in enumerate((j_far, j_left, j_right)):
-            col = text.at[pl.ds(0, 8), jj]
-            wait_for(col, tx_r.at[i])
-            send(col, col, tp_s.at[i], tp_r.at[i], frame=partner)
+        col = text.at[pl.ds(0, 8), j_far]
+        wait_for(col, tx_r.at[2])
+        send(col, col, tp_s.at[0], tp_r.at[0], frame=partner)
 
     def text_done():
         for i, jj in enumerate((j_far, j_left, j_right, j)):
             wait_for(text.at[pl.ds(0, 8), jj + shift], tp_r.at[i])
 
-    def forward(half):
-        def one(i, carry):
-            yy = (y + i) % 8
+    def forward(half, batch):
+        for d in BATCHES[batch]:
+            yy = turn(y, d, 8)
             for k in range(3):
-                jj = unit_j(half, k)
-
-                @pl.when(at(yy, jj) != frame)
-                def _():
-                    send(pack.at[half, yy, k], got.at[frame], f_s.at[half], f_r, frame=at(yy, jj))
-
-            return carry
-
-        lax.fori_loop(1, 9, one, 0)
-
+                jj = unit_j(half, yy, k)
+
+                def one():
+                    send(pack.at[half, yy, k], got.at[frame], f_s.at[half, batch], f_r, frame=at(yy, jj))
+
+                if d == 0:
+                    pl.when(j != jj)(one)
+                else:
+                    one()
+        if 0 in BATCHES[batch]:
+            @pl.when(active[half])
+            def _():
+                got[frame] = pack[half, y, my_k]
+
+    def counted(half, ref, count, sem):
         @pl.when(active[half])
         def _():
-            got[frame] = pack[half, y, my_k[half]]
-
-    def counted(half, ref, sem):
-        @pl.when(active[half])
-        def _():
-            wait_for(ref.at[pl.ds(0, 23)], sem)
+            wait_for(ref.at[pl.ds(0, count - 1)], sem)
 
         @pl.when(jnp.logical_not(active[half]))
         def _():
-            wait_for(ref.at[pl.ds(0, 24)], sem)
-
-    def forward_sent(half):
-        counted(half, got, f_s.at[half])
+            wait_for(ref.at[pl.ds(0, count)], sem)
+
+    def forward_sent(half, batch):
+        if 0 in BATCHES[batch]:
+            counted(half, got, 6, f_s.at[half, batch])
+        else:
+            wait_for(got.at[pl.ds(0, 6)], f_s.at[half, batch])
 
     def temporal(half):
         @pl.when(active[half])
@@ -193,25 +202,23 @@
 
             def one(i, carry):
                 to = (frame + i) % 64
-                send(back.at[to], backed.at[half, y * 3 + my_k[half]], b_s, b_r.at[half], frame=to)
+                send(back.at[to], backed.at[half, y * 3 + my_k], b_s, b_r.at[half], frame=to)
                 return carry
 
             lax.fori_loop(1, 64, one, 0)
-            backed[half, y * 3 + my_k[half]] = back[frame]
+            backed[half, y * 3 + my_k] = back[frame]
 
     def w_y1():
-        for i, d in ((3, 3), (2, 2), (1, 1), (4, 6), (5, 7)):
-            send(wg.at[0, j], wg.at[i, j], wy_s.at[i], wy_r.at[i], frame=at(turn(y, -d, 8), j))
-
-    def w_y2():
         for i in range(1, 6):
+            send(wg.at[0, j], wg.at[i, j], wy_s.at[i], wy_r.at[i], frame=at(turn(y, -DY[i], 8), j))
+
+    def w_y2(group):
+        first, count = GROUPS[group]
+        for i in range(first, first + count):
             wait_for(wg.at[i, j], wy_r.at[i])
-        for i, d in ((7, 2), (6, 1)):
-            send(wg.at[3, j], wg.at[i, j], wz_s.at[i - 6], wz_r.at[i - 6], frame=at(turn(y, -d, 8), j))
-
-    def w_y3():
-        for i in (6, 7):
-            wait_for(wg.at[i, j], wz_r.at[i - 6])
+            if i in (4, 5):
+                to, way = (7, 1) if i == 4 else (6, -1)
+                send(wg.at[i, j], wg.at[to, j], wy_s.at[to], wy_r.at[to], frame=at(turn(y, way, 8), j))
 
     def cut(group, jj):
         first, count = GROUPS[group]
@@ -224,13 +231,13 @@
         send(src, src, wp_s.at[0, group], wp_r.at[0, group], frame=partner)
 
     def w_x2(group):
-        src = cut(group, j_right)
-        wait_for(src, wx_r.at[1, group])
-        send(src, src, wf_s.at[group], wf_r.at[group], frame=at(y, j_left))
-        send(src, src, wp_s.at[1, group], wp_r.at[1, group], frame=partner)
-        src = cut(group, j_left)
-        wait_for(src, wx_r.at[0, group])
-        send(src, src, wp_s.at[2, group], wp_r.at[2, group], frame=partner)
+        for way, jj in ((1, j_right), (0, j_left)):
+            src = cut(group, jj)
+            wait_for(src, wx_r.at[way, group])
+            if way == ONWARD[group]:
+                to = j_left if way == 1 else j_right
+                send(src, src, wf_s.at[group], wf_r.at[group], frame=at(y, to))
+            send(src, src, wp_s.at[2 - way, group], wp_r.at[2 - way, group], frame=partner)
 
     def w_x3(group):
         src = cut(group, j_far)
@@ -274,7 +281,7 @@
         send(src, rrecv.at[at_sem], rs_s.at[at_sem], rs_r.at[at_sem], head=turn(z, 1 - 2 * way, 8))
 
     def mix(half):
-        counted(half, backed.at[half], b_r.at[half])
+        counted(half, backed.at[half], 24, b_r.at[half])
         for h in range(3):
             lanes = pl.ds(h * HD, HD)
             temp = backed[half].reshape(8, 3, 16, HD)[:, h].reshape(128, HD)
@@ -328,11 +335,9 @@
             wait_for(col, tp_s.at[i])
 
     def drain_w():
-        for i in range(1, 6):
+        for i in range(1, 8):
             wait_for(wg.at[i, j], wy_s.at[i])
-        for i in range(2):
-            wait_for(wg.at[i, j], wz_s.at[i])
-        for group in range(3):
+        for group in range(5):
             wait_for(cut(group, j), wx_s.at[0, group])
             wait_for(cut(group, j), wx_s.at[1, group])
             wait_for(cut(group, j), wf_s.at[group])
@@ -347,47 +352,70 @@
     w_y1()
     w_x1(0)
     text_y()
-    forward(0)
-    w_y2()
+    forward(0, 0)
+    forward(0, 1)
+    forward(0, 2)
+    forward(0, 3)
+    w_y2(1)
     w_x1(1)
+    w_y2(2)
+    w_x1(2)
     w_x2(0)
+    w_y2(3)
+    w_x1(3)
     text_x()
-    forward_sent(0)
-    forward(1)
-    w_y3()
-    w_x1(2)
+    forward(1, 0)
+    forward(1, 1)
+    forward(1, 2)
+    forward(1, 3)
+    temporal(0)
     w_x2(1)
+    w_x2(2)
+    w_y2(4)
+    w_x1(4)
     w_x3(0)
-    temporal(0)
+    text_x2()
+    w_x2(3)
+    w_x3(1)
+    w_x3(2)
+    w_x2(4)
+    temporal(1)
     text_p()
+    w_x3(3)
     text_done()
     spatial()
-    w_x2(2)
-    w_x3(1)
-    w_x3(2)
     w_done(0)
     w_done(1)
-    w_done(2)
     mix(0)
     project(0, 0)
+    w_x3(4)
+    w_done(2)
     project(0, 1)
+    w_done(3)
     project(0, 2)
-    project(0, 3)
-    temporal(1)
-    reduce(0, 1)
-    reduce(0, 2)
     mix(1)
     project(1, 0)
     project(1, 1)
     project(1, 2)
+    w_done(4)
+    project(0, 3)
     project(1, 3)
+    reduce(0, 1)
+    reduce(1, 1)
+    reduce(0, 2)
+    reduce(1, 2)
     reduce(0, 3)
-    reduce(1, 1)
-    reduce(1, 2)
     reduce(1, 3)
     finish(0)
     finish(1)
-    forward_sent(1)
+    forward_sent(0, 0)
+    forward_sent(0, 1)
+    forward_sent(0, 2)
+    forward_sent(0, 3)
+    forward_sent(1, 0)
+    forward_sent(1, 1)
+    forward_sent(1, 2)
+    forward_sent(1, 3)
     drain_rs(0)
     drain_rs(1)
     drain_text()
@@ -427,7 +455,7 @@
             pltpu.VMEM((2, 2, 4, 4, 2, 16, 384), BF16),
             pltpu.VMEM((2, 2, 4, 4, 2, 16, 384), BF16),
             dma((6,)),
-            dma((2,)),
+            dma((2, 4)),
             dma,
             dma,
             dma((2,)),
@@ -437,16 +465,14 @@
             dma((3,)),
             dma((4,)),
             dma((4,)),
-            dma((6,)),
-            dma((6,)),
-            dma((2,)),
-            dma((2,)),
-            dma((2, 3)),
-            dma((2, 3)),
-            dma((3,)),
-            dma((3,)),
-            dma((4, 3)),
-            dma((4, 3)),
+            dma((8,)),
+            dma((8,)),
+            dma((2, 5)),
+            dma((2, 5)),
+            dma((5,)),
+            dma((5,)),
+            dma((4, 5)),
+            dma((4, 5)),
             dma((2, 2, 4, 4)),
             dma((2, 2, 4, 4)),
         ],

time: 77.6 us -> 71.5 us (0.921)
  the two profiles are of different devices: /device:TPU:16 before, /device:TPU:1 now
where the time goes in v3:
time: 71.5 us; the launch traced here: 70.7 us
  Pallas kernels  68.4 us (96%)
  local copies, waits for them, and re-layouts  1.62 us (2%)
    pallas_call x1, Pallas kernels, per_device(): pl.pallas_call(kernel, out_shape=jax.ShapeDtypeStruct((32, 3072), BF16),...  68.4 us
    unnamed x1, local copies, waits for them, and re-layouts  1.62 us

profile of v3, /device:TPU:1, one launch (start us, length us, event | category | flops | bytes accessed | tf_op | source)
XLA Modules:
  0.0 70.7 jit_solution(1269046447858519436)
XLA Ops:
  0.7 68.4 %shard_map.82 = bf16[32,3072]{1,0:T(8,128)(2,1)} custom-call(bf16[256,384]{1,0:T(8,128)(2,1)} %q_hbm.1, bf16[256,384]{1,0:T(8,128)(2,1)} %k_hbm.1, bf16[256,384]{1,0:T(8,128)(2,1)} %v_hbm.1, bf16[4,384]{1,0:T(4,128)(2,1)} %tk_hbm.1, bf16[4,384]{1,0:T(4,128)(2,1)} %tv_hbm.1, bf16[48,384]{1,0:T(8,128)(2,1)} %bitcast.1, s32[24]{0:T(128)} %kinds_ref.1, ...), custom_call_target="tpu_custom_call" | custom-call | tf_op jit(solution)/shard_map/pallas_call | solution.py:431
  69.1 1.6 %copy.11 = bf16[32,3072]{1,0:T(8,128)(2,1)} copy(bf16[32,3072]{1,0:T(8,128)(2,1)} %shard_map.82) | data formatting | bytes 393216

commit v4 on v3

--- a/solution.py
+++ b/solution.py
@@ -276,53 +276,52 @@
         left = length(pair, way) - stage
         return turn(z, left if way == 0 else -left, 8)
 
-    def pass_on(src, half, pair, way, stage):
-        at_sem = (half, way, pair, stage)
+    def pass_on(src, pair, way, stage):
+        at_sem = (way, pair, stage)
         send(src, rrecv.at[at_sem], rs_s.at[at_sem], rs_r.at[at_sem], head=turn(z, 1 - 2 * way, 8))
 
     def mix(half):
         counted(half, backed.at[half], 24, b_r.at[half])
         for h in range(3):
             lanes = pl.ds(h * HD, HD)
-            temp = backed[half].reshape(8, 3, 16, HD)[:, h].reshape(128, HD)
-            own = spat[:, half, :, lanes].reshape(128, HD)
-            mixed[half, :, lanes] = jnp.where(kinds_ref[z * 3 + h] == 1, temp, own)
-
-    def project(half, pair):
+            temp = backed[half].reshape(8, 3, 16, HD)[:, h]
+            mixed[:, half, :, lanes] = jnp.where(kinds_ref[z * 3 + h] == 1, temp, spat[:, half, :, lanes])
+
+    def project(pair):
         for i in range(2):
-            term = dot(mixed[half], wg[pair * 2 + i].reshape(384, 384), NT)
-            part[half, pair, :, i] = term.astype(BF16).reshape(8, 16, 384)
+            term = dot(mixed[...].reshape(256, 384), wg[pair * 2 + i].reshape(384, 384), NT)
+            part[pair, :, i] = term.astype(BF16).reshape(8, 32, 384)
         for way in range(2):
-            pass_on(part.at[half, pair, dest(pair, way, 0)], half, pair, way, 0)
-
-    def reduce(half, stage):
+            pass_on(part.at[pair, dest(pair, way, 0)], pair, way, 0)
+
+    def reduce(stage):
         for pair in range(4):
             for way in range(2):
                 if stage < length(pair, way):
-                    before = (half, way, pair, stage - 1)
-                    now = (half, way, pair, stage)
+                    before = (way, pair, stage - 1)
+                    now = (way, pair, stage)
                     wait_for(rrecv.at[before], rs_r.at[before])
-                    own = part[half, pair, dest(pair, way, stage)].astype(F32)
+                    own = part[pair, dest(pair, way, stage)].astype(F32)
                     rsend[now] = (own + rrecv[before].astype(F32)).astype(BF16)
-                    pass_on(rsend.at[now], half, pair, way, stage)
-
-    def finish(half):
+                    pass_on(rsend.at[now], pair, way, stage)
+
+    def finish():
         for pair in range(4):
-            own = part[half, pair, z].astype(F32)
+            own = part[pair, z].astype(F32)
             for way in range(2):
-                last = (half, way, pair, length(pair, way) - 1)
+                last = (way, pair, length(pair, way) - 1)
                 wait_for(rrecv.at[last], rs_r.at[last])
                 own = own + rrecv[last].astype(F32)
             for i in range(2):
                 block = turn(y, DY[pair * 2 + i], 8)
                 columns = pl.ds(pl.multiple_of(block * 384, 384), 384)
-                out_ref[half * 16:(half + 1) * 16, columns] = own[i].astype(BF16)
-
-    def drain_rs(half):
+                out_ref[:, columns] = own[i].astype(BF16)
+
+    def drain_rs():
         for pair in range(4):
             for way in range(2):
                 for stage in range(length(pair, way)):
-                    now = (half, way, pair, stage)
+                    now = (way, pair, stage)
                     wait_for(rrecv.at[now], rs_s.at[now])
 
     def drain_text():
@@ -360,14 +359,14 @@
     w_x1(1)
     w_y2(2)
     w_x1(2)
+    forward(1, 0)
+    forward(1, 1)
+    forward(1, 2)
+    forward(1, 3)
     w_x2(0)
     w_y2(3)
     w_x1(3)
     text_x()
-    forward(1, 0)
-    forward(1, 1)
-    forward(1, 2)
-    forward(1, 3)
     temporal(0)
     w_x2(1)
     w_x2(2)
@@ -384,30 +383,22 @@
     w_x3(3)
     text_done()
     spatial()
+    mix(0)
     w_done(0)
     w_done(1)
-    mix(0)
-    project(0, 0)
     w_x3(4)
+    mix(1)
+    project(0)
     w_done(2)
-    project(0, 1)
+    project(1)
     w_done(3)
-    project(0, 2)
-    mix(1)
-    project(1, 0)
-    project(1, 1)
-    project(1, 2)
+    project(2)
     w_done(4)
-    project(0, 3)
-    project(1, 3)
-    reduce(0, 1)
-    reduce(1, 1)
-    reduce(0, 2)
-    reduce(1, 2)
-    reduce(0, 3)
-    reduce(1, 3)
-    finish(0)
-    finish(1)
+    project(3)
+    reduce(1)
+    reduce(2)
+    reduce(3)
+    finish()
     forward_sent(0, 0)
     forward_sent(0, 1)
     forward_sent(0, 2)
@@ -416,8 +407,7 @@
     forward_sent(1, 1)
     forward_sent(1, 2)
     forward_sent(1, 3)
-    drain_rs(0)
-    drain_rs(1)
+    drain_rs()
     drain_text()
     drain_w()
     drain_back()
@@ -450,10 +440,10 @@
             pltpu.VMEM((8, 8, 32, HD), BF16),
             pltpu.VMEM((6, 256, HD), BF16),
             pltpu.VMEM((8, 2, 16, 384), BF16),
-            pltpu.VMEM((2, 128, 384), BF16),
-            pltpu.VMEM((2, 4, 8, 2, 16, 384), BF16),
-            pltpu.VMEM((2, 2, 4, 4, 2, 16, 384), BF16),
-            pltpu.VMEM((2, 2, 4, 4, 2, 16, 384), BF16),
+            pltpu.VMEM((8, 2, 16, 384), BF16),
+            pltpu.VMEM((4, 8, 2, 32, 384), BF16),
+            pltpu.VMEM((2, 4, 4, 2, 32, 384), BF16),
+            pltpu.VMEM((2, 4, 4, 2, 32, 384), BF16),
             dma((6,)),
             dma((2, 4)),
             dma,
@@ -473,8 +463,8 @@
             dma((5,)),
             dma((4, 5)),
             dma((4, 5)),
-            dma((2, 2, 4, 4)),
-            dma((2, 2, 4, 4)),
+            dma((2, 4, 4)),
+            dma((2, 4, 4)),
         ],
         compiler_params=pltpu.CompilerParams(
             collective_id=0, has_side_effects=True, vmem_limit_bytes=60 * 1024 * 1024

time: 71.5 us -> 72 us (level)
  Pallas kernels: 68.4 us -> 69.5 us
    pallas_call x1, Pallas kernels: 68.4 us -> 69.5 us  [per_device(): pl.pallas_call(kernel, out_shape=jax.ShapeDtypeStruct((32, 3072), BF16),...]
where the time goes in v4:
time: 72 us; the launch traced here: 71.8 us
  Pallas kernels  69.5 us (97%)
  local copies, waits for them, and re-layouts  1.62 us (2%)
    pallas_call x1, Pallas kernels, per_device(): pl.pallas_call(kernel, out_shape=jax.ShapeDtypeStruct((32, 3072), BF16),...  69.5 us
    unnamed x1, local copies, waits for them, and re-layouts  1.62 us

profile of v4, /device:TPU:1, one launch (start us, length us, event | category | flops | bytes accessed | tf_op | source)
XLA Modules:
  0.0 71.8 jit_solution(13268728652357275176)
XLA Ops:
  0.7 69.5 %shard_map.82 = bf16[32,3072]{1,0:T(8,128)(2,1)} custom-call(bf16[256,384]{1,0:T(8,128)(2,1)} %q_hbm.1, bf16[256,384]{1,0:T(8,128)(2,1)} %k_hbm.1, bf16[256,384]{1,0:T(8,128)(2,1)} %v_hbm.1, bf16[4,384]{1,0:T(4,128)(2,1)} %tk_hbm.1, bf16[4,384]{1,0:T(4,128)(2,1)} %tv_hbm.1, bf16[48,384]{1,0:T(8,128)(2,1)} %bitcast.1, s32[24]{0:T(128)} %kinds_ref.1, ...), custom_call_target="tpu_custom_call" | custom-call | tf_op jit(solution)/shard_map/pallas_call | solution.py:421
  70.2 1.6 %copy.11 = bf16[32,3072]{1,0:T(8,128)(2,1)} copy(bf16[32,3072]{1,0:T(8,128)(2,1)} %shard_map.82) | data formatting | bytes 393216

commit v5 on v3

--- a/solution.py
+++ b/solution.py
@@ -360,14 +360,14 @@
     w_x1(1)
     w_y2(2)
     w_x1(2)
+    forward(1, 0)
+    forward(1, 1)
+    forward(1, 2)
+    forward(1, 3)
     w_x2(0)
     w_y2(3)
     w_x1(3)
     text_x()
-    forward(1, 0)
-    forward(1, 1)
-    forward(1, 2)
-    forward(1, 3)
     temporal(0)
     w_x2(1)
     w_x2(2)

time: 71.5 us -> 71.5 us (level)
  no operation moved by 1% of the time
where the time goes in v5:
time: 71.5 us; the launch traced here: 70.3 us
  Pallas kernels  68 us (95%)
  local copies, waits for them, and re-layouts  1.62 us (2%)
    pallas_call x1, Pallas kernels, per_device(): pl.pallas_call(kernel, out_shape=jax.ShapeDtypeStruct((32, 3072), BF16),...  68 us
    unnamed x1, local copies, waits for them, and re-layouts  1.62 us

profile of v5, /device:TPU:1, one launch (start us, length us, event | category | flops | bytes accessed | tf_op | source)
XLA Modules:
  0.0 70.3 jit_solution(1249807140807368368)
XLA Ops:
  0.7 68.0 %shard_map.82 = bf16[32,3072]{1,0:T(8,128)(2,1)} custom-call(bf16[256,384]{1,0:T(8,128)(2,1)} %q_hbm.1, bf16[256,384]{1,0:T(8,128)(2,1)} %k_hbm.1, bf16[256,384]{1,0:T(8,128)(2,1)} %v_hbm.1, bf16[4,384]{1,0:T(4,128)(2,1)} %tk_hbm.1, bf16[4,384]{1,0:T(4,128)(2,1)} %tv_hbm.1, bf16[48,384]{1,0:T(8,128)(2,1)} %bitcast.1, s32[24]{0:T(128)} %kinds_ref.1, ...), custom_call_target="tpu_custom_call" | custom-call | tf_op jit(solution)/shard_map/pallas_call | solution.py:431
  68.7 1.6 %copy.11 = bf16[32,3072]{1,0:T(8,128)(2,1)} copy(bf16[32,3072]{1,0:T(8,128)(2,1)} %shard_map.82) | data formatting | bytes 393216
